TPU v7x, 32 devices: a whole 2x2x4 slice. The times are simulated.
32 devices in a mesh: pipe: 2 (over core), seq: 4 (over z), chan: 4 (over y, x).
Axes of the slice: x: 2, y: 2, z: 4, core: 2. Of those that a mesh axis runs over, the one named last changes fastest.
Arguments:
- grad_out: bfloat16 [2, 1024, 2048], P('pipe', 'seq', 'chan'), may hold values from -6 to 6
- value_branch: bfloat16 [2, 1024, 2048], P('pipe', 'seq', 'chan'), may hold values from -0.1875 to 0.1875
- key_gate: bfloat16 [2, 1024, 2048], P('pipe', 'seq', 'chan'), may hold values from -6 to 6
- query_gate: bfloat16 [2, 1024, 2048], P('pipe', 'seq', 'chan'), may hold values from -6 to 6
- short_weights: float32 [2, 3, 2048], P('pipe', None, 'chan'), may hold values from -3 to 3
- long_filters: bfloat16 [2, 1024, 2048], P('pipe', 'seq', 'chan'), may hold values from -0.1875 to 0.1875
Outputs:
- passed_grad: bfloat16 [2, 1024, 2048], P('pipe', 'seq', 'chan')
- filter_grad: float32 [2, 1024, 2048], P('pipe', 'seq', 'chan')
All inputs are finite; a program needn't handle non-finite values.
Results may differ from a plain program's by a relative error of at most 0.0049.
Values may be sent and summed in bfloat16 or wider, within the bound.
A program may use at most 64 MiB of HBM per device.

v0:
```python
import functools
import math

import jax
import jax.numpy as jnp
import numpy as np
from jax import lax
from jax.experimental import pallas as pl
from jax.experimental.pallas import tpu as pltpu
from jax.sharding import PartitionSpec as P


def from_behind(value, axis, by):
    devices = lax.axis_size(axis)
    pairs = [(i, i + by) for i in range(devices) if 0 <= i + by < devices]
    return lax.ppermute(value, axis, pairs)


def shifted(block, axis, distance):
    devices = range(lax.axis_size(axis))
    route = [((i - distance) % len(devices), i) for i in devices]
    return lax.ppermute(block, axis, route)


def phase_table(product, modulus):
    angles = (product % modulus).astype(jnp.float32) * (2.0 * math.pi / modulus)
    return (jnp.cos(angles), jnp.sin(angles))


def contract(form, table, values):
    return jnp.einsum(form, table, values, precision=lax.Precision.HIGHEST)


def forward_blocks(signal, row_first, padded):
    block_count = signal.shape[0]
    row_count = signal.shape[1]
    frequency = jnp.arange(2 * block_count, dtype=jnp.int32)
    block_index = jnp.arange(block_count, dtype=jnp.int32)
    cos_table, sin_table = phase_table(frequency[:, None] * block_index[None, :], 2 * block_count)
    real_part = contract("ca,arx->crx", cos_table, signal)
    imag_part = -contract("ca,arx->crx", sin_table, signal)
    row_index = row_first + jnp.arange(row_count, dtype=jnp.int32)
    cos_twist, sin_twist = phase_table(frequency[:, None] * row_index[None, :], padded)
    cos_twist = cos_twist[:, :, None]
    sin_twist = sin_twist[:, :, None]
    return (
        real_part * cos_twist + imag_part * sin_twist,
        imag_part * cos_twist - real_part * sin_twist,
    )


def along_rows(real_part, imag_part, direction):
    length = real_part.shape[1]
    indices = jnp.arange(length, dtype=jnp.int32)
    cos_table, sin_table = phase_table(indices[:, None] * indices[None, :], length)
    cos_real = contract("dr,crx->cdx", cos_table, real_part)
    cos_imag = contract("dr,crx->cdx", cos_table, imag_part)
    sin_real = contract("dr,crx->cdx", sin_table, real_part)
    sin_imag = contract("dr,crx->cdx", sin_table, imag_part)
    return (cos_real - direction * sin_imag, cos_imag + direction * sin_real)


def inverse_twist(real_part, imag_part, freq_first, padded):
    frequency = freq_first + jnp.arange(real_part.shape[0], dtype=jnp.int32)
    row_index = jnp.arange(real_part.shape[1], dtype=jnp.int32)
    cos_twist, sin_twist = phase_table(frequency[:, None] * row_index[None, :], padded)
    cos_twist = cos_twist[:, :, None]
    sin_twist = sin_twist[:, :, None]
    return (
        real_part * cos_twist - imag_part * sin_twist,
        imag_part * cos_twist + real_part * sin_twist,
    )


def inverse_blocks(real_part, imag_part, padded):
    block_count = real_part.shape[0] // 2
    block_index = jnp.arange(block_count, dtype=jnp.int32)
    frequency = jnp.arange(2 * block_count, dtype=jnp.int32)
    cos_table, sin_table = phase_table(block_index[:, None] * frequency[None, :], 2 * block_count)
    summed = contract("ac,crx->arx", cos_table, real_part) - contract(
        "ac,crx->arx", sin_table, imag_part
    )
    return summed * (1.0 / padded)


def spectral_products(conv_real, conv_imag, gated_real, gated_imag, filter_real, filter_imag):
    back_real = conv_real * filter_real + conv_imag * filter_imag
    back_imag = conv_imag * filter_real - conv_real * filter_imag
    fold_real = conv_real * gated_real + conv_imag * gated_imag
    fold_imag = conv_imag * gated_real - conv_real * gated_imag
    return (back_real, back_imag, fold_real, fold_imag)


def spread_body(grad_out, value_branch, key_gate, query_gate, short_weights, long_filters):
    grad_y = grad_out[0]
    tok_rows, columns = grad_y.shape
    devices = lax.axis_size("seq")
    position = lax.axis_index("seq")
    padded = 2 * tok_rows * devices
    key_values = key_gate[0].astype(jnp.float32)
    grad_conv = (query_gate[0].astype(jnp.float32) * grad_y.astype(jnp.float32)).astype(
        jnp.bfloat16
    )
    gated_value = (key_values * value_branch[0].astype(jnp.float32)).astype(jnp.bfloat16)
    per_device = tok_rows // devices
    pieces = (
        lax.all_to_all(grad_conv[None], "seq", split_axis=1, concat_axis=0, tiled=True),
        lax.all_to_all(gated_value[None], "seq", split_axis=1, concat_axis=0, tiled=True),
        lax.all_to_all(long_filters, "seq", split_axis=1, concat_axis=0, tiled=True),
    )
    halves = [
        forward_blocks(piece.astype(jnp.float32), position * per_device, padded) for piece in pieces
    ]
    exchanged = (
        lax.all_to_all(halves[0][0], "seq", split_axis=0, concat_axis=1, tiled=True),
        lax.all_to_all(halves[0][1], "seq", split_axis=0, concat_axis=1, tiled=True),
        lax.all_to_all(halves[1][0], "seq", split_axis=0, concat_axis=1, tiled=True),
        lax.all_to_all(halves[1][1], "seq", split_axis=0, concat_axis=1, tiled=True),
        lax.all_to_all(halves[2][0], "seq", split_axis=0, concat_axis=1, tiled=True),
        lax.all_to_all(halves[2][1], "seq", split_axis=0, concat_axis=1, tiled=True),
    )
    conv_real, conv_imag = along_rows(exchanged[0], exchanged[1], -1.0)
    gated_real, gated_imag = along_rows(exchanged[2], exchanged[3], -1.0)
    filter_real, filter_imag = along_rows(exchanged[4], exchanged[5], -1.0)
    back_real, back_imag, fold_real, fold_imag = spectral_products(
        conv_real, conv_imag, gated_real, gated_imag, filter_real, filter_imag
    )
    pair_count = fold_real.shape[0]
    back_real, back_imag = along_rows(back_real, back_imag, 1.0)
    back_real, back_imag = inverse_twist(back_real, back_imag, position * pair_count, padded)
    fold_real, fold_imag = along_rows(fold_real, fold_imag, 1.0)
    fold_real, fold_imag = inverse_twist(fold_real, fold_imag, position * pair_count, padded)
    returned = (
        lax.all_to_all(back_real, "seq", split_axis=1, concat_axis=0, tiled=True),
        lax.all_to_all(back_imag, "seq", split_axis=1, concat_axis=0, tiled=True),
        lax.all_to_all(fold_real, "seq", split_axis=1, concat_axis=0, tiled=True),
        lax.all_to_all(fold_imag, "seq", split_axis=1, concat_axis=0, tiled=True),
    )
    settled = (
        lax.all_to_all(
            inverse_blocks(returned[0], returned[1], padded),
            "seq",
            split_axis=0,
            concat_axis=1,
            tiled=True,
        ),
        lax.all_to_all(
            inverse_blocks(returned[2], returned[3], padded),
            "seq",
            split_axis=0,
            concat_axis=1,
            tiled=True,
        ),
    )
    grad_gated = settled[0][0]
    grad_filter = settled[1][0]
    grad_value = key_values * grad_gated
    next_rim = from_behind(grad_value[:2], "seq", -1)
    longer = jnp.concatenate([grad_value, next_rim], axis=0)
    weights = short_weights[0]
    grad_input = (
        weights[0] * longer[:tok_rows]
        + weights[1] * longer[1 : tok_rows + 1]
        + weights[2] * longer[2:]
    )
    passed = shifted(grad_input.astype(jnp.bfloat16)[None], "pipe", -1)
    return (passed, grad_filter[None])


LANES = 128
RIM = 16
MESH = pl.DeviceIdType.MESH


def half_step_tables(tokens):
    odd = 2 * np.arange(tokens, dtype=np.int64)[:, None] + 1
    turns = (odd * np.arange(tokens, dtype=np.int64)[None, :]) % (4 * tokens)
    angles = turns * (2.0 * np.pi / (4 * tokens))
    forward = np.concatenate([np.cos(angles), np.sin(angles)], axis=0)
    pairs = []
    for table in (forward, forward.T):
        high = table.astype(jnp.bfloat16)
        low = (table - high.astype(np.float64)).astype(jnp.bfloat16)
        pairs += [high, low]
    return pairs


def relay_kernel(
    devices, go, vb, kg, qg, sw, lf, fwd_hi_hbm, fwd_lo_hbm, inv_hi_hbm, inv_lo_hbm,
    passed, fold_out,
    conv_src, gated_src, conv_all, filt_all, gated_all, fwd_hi, fwd_lo, inv_hi, inv_lo,
    spec_conv, spec_other, packed, back_src, fold_src, back_got, fold_got, key_got, weight_got,
    table_sem, own_sem, send_sem, recv_sem, back_send, back_recv, side_send, side_recv,
):
    rows = go.shape[1]
    tokens = rows * devices
    pipe = lax.axis_index("pipe")
    me = lax.axis_index("seq")
    other = 1 - pipe

    tables = [
        pltpu.make_async_copy(source, target, table_sem.at[i])
        for i, (source, target) in enumerate(
            ((fwd_hi_hbm, fwd_hi), (fwd_lo_hbm, fwd_lo), (inv_hi_hbm, inv_hi), (inv_lo_hbm, inv_lo))
        )
    ]

    def peer(distance):
        return lax.rem(me + distance, devices)

    barrier = pltpu.get_barrier_semaphore()
    for distance in range(devices):
        if distance:
            pl.semaphore_signal(
                barrier, inc=1, device_id={"pipe": pipe, "seq": peer(distance)}, device_id_type=MESH
            )
        pl.semaphore_signal(
            barrier, inc=1, device_id={"pipe": other, "seq": peer(distance)}, device_id_type=MESH
        )
    for copy in tables:
        copy.start()
    conv_src[...] = (qg[0].astype(jnp.float32) * go[0].astype(jnp.float32)).astype(jnp.bfloat16)
    gated_src[...] = (kg[0].astype(jnp.float32) * vb[0].astype(jnp.float32)).astype(jnp.bfloat16)
    back_src[pl.ds(tokens, RIM), :] = jnp.zeros((RIM, LANES), jnp.bfloat16)
    pl.semaphore_wait(barrier, 2 * devices - 1)

    def lanes_of(device):
        return pl.ds(pl.multiple_of(device * LANES, LANES), LANES)

    def rows_of(device, extra=0):
        return pl.ds(pl.multiple_of(device * rows, rows), rows + extra)

    def scatter(kind, source, target):
        own = pltpu.make_async_copy(
            source.at[:, lanes_of(me)], target.at[rows_of(me)], own_sem.at[kind]
        )
        own.start()
        copies = []
        for distance in range(1, devices):
            copy = pltpu.make_async_remote_copy(
                src_ref=source.at[:, lanes_of(peer(distance))],
                dst_ref=target.at[rows_of(me)],
                send_sem=send_sem.at[kind, distance],
                recv_sem=recv_sem.at[kind, distance],
                device_id={"pipe": pipe, "seq": peer(distance)},
                device_id_type=MESH,
            )
            copy.start()
            copies.append(copy)
        return own, copies

    def landed(group):
        own, copies = group
        own.wait()
        for copy in copies:
            copy.wait_recv()

    filt_group = scatter(0, lf.at[0], filt_all)
    conv_group = scatter(1, conv_src, conv_all)
    gated_group = scatter(2, gated_src, gated_all)
    side = []
    for i, (source, target, at) in enumerate(
        (
            (kg.at[0], key_got.at[pl.ds(0, rows)], me),
            (kg.at[0, pl.ds(0, RIM)], key_got.at[pl.ds(rows, RIM)], peer(devices - 1)),
            (sw.at[0], weight_got, me),
        )
    ):
        copy = pltpu.make_async_remote_copy(
            src_ref=source, dst_ref=target, send_sem=side_send.at[i], recv_sem=side_recv.at[i],
            device_id={"pipe": other, "seq": at}, device_id_type=MESH,
        )
        copy.start()
        side.append(copy)

    step = tokens // 2

    def transform(signal, target):
        @pl.loop(0, 2 * tokens // step)
        def _(part):
            at = pl.ds(pl.multiple_of(part * step, step), step)
            values = signal[...]
            target[at, :] = jnp.dot(
                fwd_hi[at, :], values, preferred_element_type=jnp.float32
            ) + jnp.dot(fwd_lo[at, :], values, preferred_element_type=jnp.float32)

    def pack(at, value):
        high = value.astype(jnp.bfloat16)
        packed[at, pl.ds(0, LANES)] = high
        packed[at, pl.ds(LANES, LANES)] = (value - high.astype(jnp.float32)).astype(jnp.bfloat16)

    def correlate(target):
        chunk = rows

        @pl.loop(0, tokens // chunk)
        def _(part):
            top = pl.ds(pl.multiple_of(part * chunk, chunk), chunk)
            low = pl.ds(pl.multiple_of(tokens + part * chunk, chunk), chunk)
            conv_cos, conv_sin = spec_conv[top, :], spec_conv[low, :]
            other_cos, other_sin = spec_other[top, :], spec_other[low, :]
            scale = 1.0 / tokens
            pack(top, (conv_cos * other_cos + conv_sin * other_sin) * scale)
            pack(low, (conv_sin * other_cos - conv_cos * other_sin) * scale)

        @pl.loop(0, tokens // chunk)
        def _(part):
            at = pl.ds(pl.multiple_of(part * chunk, chunk), chunk)
            wide = jnp.dot(inv_hi[at, :], packed[...], preferred_element_type=jnp.float32)
            narrow = jnp.dot(
                inv_lo[at, :], packed[:, pl.ds(0, LANES)], preferred_element_type=jnp.float32
            )
            target[at, :] = (wide[:, :LANES] + wide[:, LANES:] + narrow).astype(jnp.bfloat16)

    landed(filt_group)
    tables[0].wait()
    tables[1].wait()
    transform(filt_all, spec_other)
    landed(conv_group)
    transform(conv_all, spec_conv)
    tables[2].wait()
    tables[3].wait()
    correlate(back_src)
    backs = []
    for distance in range(devices):
        copy = pltpu.make_async_remote_copy(
            src_ref=back_src.at[rows_of(peer(distance), RIM)],
            dst_ref=back_got.at[me],
            send_sem=back_send.at[distance],
            recv_sem=back_recv.at[distance],
            device_id={"pipe": other, "seq": peer(distance)},
            device_id_type=MESH,
        )
        copy.start()
        backs.append(copy)

    landed(gated_group)
    transform(gated_all, spec_other)
    correlate(fold_src)
    own = pltpu.make_async_copy(fold_src.at[rows_of(me)], fold_got.at[me], own_sem.at[3])
    own.start()
    folds = []
    for distance in range(1, devices):
        copy = pltpu.make_async_remote_copy(
            src_ref=fold_src.at[rows_of(peer(distance))],
            dst_ref=fold_got.at[me],
            send_sem=send_sem.at[3, distance],
            recv_sem=recv_sem.at[3, distance],
            device_id={"pipe": pipe, "seq": peer(distance)},
            device_id_type=MESH,
        )
        copy.start()
        folds.append(copy)

    for copy in side + backs:
        copy.wait_recv()
    for block in range(devices):
        columns = pl.ds(block * LANES, LANES)
        value = key_got[:, columns].astype(jnp.float32) * back_got[block].astype(jnp.float32)
        extent = rows + RIM
        total = weight_got[pl.ds(0, 1), columns] * value
        total += weight_got[pl.ds(1, 1), columns] * pltpu.roll(value, extent - 1, 0)
        total += weight_got[pl.ds(2, 1), columns] * pltpu.roll(value, extent - 2, 0)
        passed[0, :, columns] = total[:rows].astype(jnp.bfloat16)
    own.wait()
    for copy in folds:
        copy.wait_recv()
    for block in range(devices):
        fold_out[0, :, pl.ds(block * LANES, LANES)] = fold_got[block].astype(jnp.float32)
    for copy in filt_group[1] + conv_group[1] + gated_group[1] + side + backs + folds:
        copy.wait_send()


def relay_body(grad_out, value_branch, key_gate, query_gate, short_weights, long_filters):
    _, rows, columns = grad_out.shape
    devices = lax.axis_size("seq")
    tokens = rows * devices
    tables = [jnp.asarray(table) for table in half_step_tables(tokens)]
    vmem = pl.BlockSpec(memory_space=pltpu.VMEM)
    anywhere = pl.BlockSpec(memory_space=pl.ANY)
    half, full = jnp.bfloat16, jnp.float32
    return pl.pallas_call(
        functools.partial(relay_kernel, devices),
        out_shape=(
            jax.ShapeDtypeStruct((1, rows, columns), half),
            jax.ShapeDtypeStruct((1, rows, columns), full),
        ),
        in_specs=[vmem] * 6 + [anywhere] * 4,
        out_specs=(vmem, vmem),
        scratch_shapes=[
            pltpu.VMEM((rows, columns), half),
            pltpu.VMEM((rows, columns), half),
            pltpu.VMEM((tokens, LANES), half),
            pltpu.VMEM((tokens, LANES), half),
            pltpu.VMEM((tokens, LANES), half),
            pltpu.VMEM((2 * tokens, tokens), half),
            pltpu.VMEM((2 * tokens, tokens), half),
            pltpu.VMEM((tokens, 2 * tokens), half),
            pltpu.VMEM((tokens, 2 * tokens), half),
            pltpu.VMEM((2 * tokens, LANES), full),
            pltpu.VMEM((2 * tokens, LANES), full),
            pltpu.VMEM((2 * tokens, 2 * LANES), half),
            pltpu.VMEM((tokens + RIM, LANES), half),
            pltpu.VMEM((tokens, LANES), half),
            pltpu.VMEM((devices, rows + RIM, LANES), half),
            pltpu.VMEM((devices, rows, LANES), half),
            pltpu.VMEM((rows + RIM, columns), half),
            pltpu.VMEM((3, columns), full),
            pltpu.SemaphoreType.DMA((4,)),
            pltpu.SemaphoreType.DMA((4,)),
            pltpu.SemaphoreType.DMA((4, devices)),
            pltpu.SemaphoreType.DMA((4, devices)),
            pltpu.SemaphoreType.DMA((devices,)),
            pltpu.SemaphoreType.DMA((devices,)),
            pltpu.SemaphoreType.DMA((3,)),
            pltpu.SemaphoreType.DMA((3,)),
        ],
        compiler_params=pltpu.CompilerParams(
            collective_id=0, has_side_effects=True, vmem_limit_bytes=44 * 2**20
        ),
        cost_estimate=pl.CostEstimate(
            flops=28 * tokens * tokens * LANES, bytes_accessed=16 * tokens * tokens, transcendentals=0
        ),
    )(grad_out, value_branch, key_gate, query_gate, short_weights, long_filters, *tables)


def solution(mesh):
    placed = (
        P("pipe", "seq", "chan"),
        P("pipe", "seq", "chan"),
        P("pipe", "seq", "chan"),
        P("pipe", "seq", "chan"),
        P("pipe", None, "chan"),
        P("pipe", "seq", "chan"),
    )

    def run(*arrays):
        _, tokens, channels = arrays[0].shape
        devices = mesh.shape["seq"]
        fits = (
            mesh.shape["pipe"] == 2
            and devices > 1
            and channels == mesh.shape["chan"] * devices * LANES
            and tokens <= 1024
            and tokens % (devices * RIM) == 0
        )
        return jax.shard_map(
            relay_body if fits else spread_body,
            mesh=mesh,
            in_specs=placed,
            out_specs=(P("pipe", "seq", "chan"), P("pipe", "seq", "chan")),
            check_vma=False,
        )(*arrays)

    return run
```

profile of v0, /device:TPU:0, one launch (start us, length us, event | category | flops | bytes accessed | tf_op | source)
XLA Modules:
  0.0 48.7 jit_solution(9292720728294355142)
XLA Ops:
  0.6 0.7 %copy.12.sw = f32[1,3,512]{2,1,0:T(4,128)S(1)} copy(f32[1,3,512]{2,0,1:T(1,128)} %param.14) | data formatting | bytes 12288 | tf_op args[4]
  1.3 0.0 copy-start
  1.3 2.2 %copy-done = bf16[2048,1024]{1,0:T(8,128)(2,1)S(1)} copy-done((bf16[2048,1024]{1,0:T(8,128)(2,1)S(1)}, bf16[2048,1024]{1,0:T(8,128)(2,1)}, u32[]{:S(2)}) %copy-start) | copy-done | bytes 4194328
  3.5 0.0 copy-start.1
  3.5 0.9 %copy-done.1 = bf16[1,256,512]{2,1,0:T(8,128)(2,1)S(1)} copy-done((bf16[1,256,512]{2,1,0:T(8,128)(2,1)S(1)}, bf16[1,256,512]{2,1,0:T(8,128)(2,1)}, u32[]{:S(2)}) %copy-start.1) | copy-done | bytes 262168
  4.5 0.0 copy-start.2
  4.5 0.9 %copy-done.2 = bf16[1,256,512]{2,1,0:T(8,128)(2,1)S(1)} copy-done((bf16[1,256,512]{2,1,0:T(8,128)(2,1)S(1)}, bf16[1,256,512]{2,1,0:T(8,128)(2,1)}, u32[]{:S(2)}) %copy-start.2) | copy-done | bytes 262168
  5.4 0.0 copy-start.3
  5.4 0.9 %copy-done.3 = bf16[1,256,512]{2,1,0:T(8,128)(2,1)S(1)} copy-done((bf16[1,256,512]{2,1,0:T(8,128)(2,1)S(1)}, bf16[1,256,512]{2,1,0:T(8,128)(2,1)}, u32[]{:S(2)}) %copy-start.3) | copy-done | bytes 262168
  6.4 0.0 copy-start.4
  6.4 0.9 %copy-done.4 = bf16[1,256,512]{2,1,0:T(8,128)(2,1)S(1)} copy-done((bf16[1,256,512]{2,1,0:T(8,128)(2,1)S(1)}, bf16[1,256,512]{2,1,0:T(8,128)(2,1)}, u32[]{:S(2)}) %copy-start.4) | copy-done | bytes 262168
  7.3 0.0 copy-start.5
  7.3 0.9 %copy-done.5 = bf16[1,256,512]{2,1,0:T(8,128)(2,1)S(1)} copy-done((bf16[1,256,512]{2,1,0:T(8,128)(2,1)S(1)}, bf16[1,256,512]{2,1,0:T(8,128)(2,1)}, u32[]{:S(2)}) %copy-start.5) | copy-done | bytes 262168
  8.3 38.9 %shard_map.113 = (bf16[1,256,512]{2,1,0:T(8,128)(2,1)S(1)}, f32[1,256,512]{2,1,0:T(8,128)S(1)}) custom-call(bf16[1,256,512]{2,1,0:T(8,128)(2,1)S(1)} %copy-done.1, bf16[1,256,512]{2,1,0:T(8,128)(2,1)S(1)} %copy-done.2, bf16[1,256,512]{2,1,0:T(8,128)(2,1)S(1)} %copy-done.3, bf16[1,256,512]{2,1,0:T(8,128)(2,1)S(1)} %copy-done.4, f32[1,3,512]{2,1,0:T(4,128)S(1)} %copy.12.sw, ...), custom_call_target="tpu_custom_call" | custom-call | flops 3758096384 | bytes 16777216 | tf_op jit(solution)/shard_map/pallas_call | solution.py:381
  47.2 0.7 %copy.15 = bf16[1,256,512]{2,1,0:T(8,128)(2,1)} copy(bf16[1,256,512]{2,1,0:T(8,128)(2,1)S(1)} %get-tuple-element.4) | data formatting | bytes 524288
  47.9 0.8 %copy.16 = f32[1,256,512]{2,1,0:T(8,128)} copy(f32[1,256,512]{2,1,0:T(8,128)S(1)} %get-tuple-element.5) | data formatting | bytes 1048576
Async XLA Ops:
  1.3 2.2 %copy-start = (bf16[2048,1024]{1,0:T(8,128)(2,1)S(1)}, bf16[2048,1024]{1,0:T(8,128)(2,1)}, u32[]{:S(2)}) copy-start(bf16[2048,1024]{1,0:T(8,128)(2,1)} %constant.8.clone.fwd_hi_hbm) | copy-start | bytes 12582916
  3.5 0.9 %copy-start.1 = (bf16[1,256,512]{2,1,0:T(8,128)(2,1)S(1)}, bf16[1,256,512]{2,1,0:T(8,128)(2,1)}, u32[]{:S(2)}) copy-start(bf16[1,256,512]{2,1,0:T(8,128)(2,1)} %go.1) | copy-start | bytes 786436
  4.5 0.9 %copy-start.2 = (bf16[1,256,512]{2,1,0:T(8,128)(2,1)S(1)}, bf16[1,256,512]{2,1,0:T(8,128)(2,1)}, u32[]{:S(2)}) copy-start(bf16[1,256,512]{2,1,0:T(8,128)(2,1)} %vb.1) | copy-start | bytes 786436
  5.4 0.9 %copy-start.3 = (bf16[1,256,512]{2,1,0:T(8,128)(2,1)S(1)}, bf16[1,256,512]{2,1,0:T(8,128)(2,1)}, u32[]{:S(2)}) copy-start(bf16[1,256,512]{2,1,0:T(8,128)(2,1)} %kg.1) | copy-start | bytes 786436
  6.4 0.9 %copy-start.4 = (bf16[1,256,512]{2,1,0:T(8,128)(2,1)S(1)}, bf16[1,256,512]{2,1,0:T(8,128)(2,1)}, u32[]{:S(2)}) copy-start(bf16[1,256,512]{2,1,0:T(8,128)(2,1)} %qg.1) | copy-start | bytes 786436
  7.3 0.9 %copy-start.5 = (bf16[1,256,512]{2,1,0:T(8,128)(2,1)S(1)}, bf16[1,256,512]{2,1,0:T(8,128)(2,1)}, u32[]{:S(2)}) copy-start(bf16[1,256,512]{2,1,0:T(8,128)(2,1)} %lf.1) | copy-start | bytes 786436
where the time goes:
time: 49 us; the launch traced here: 48.7 us
  Pallas kernels  38.9 us (79%)
  local copies, waits for them, and re-layouts  9.13 us (19%)
  between operations  0.64 us (1%)
    pallas_call x1, Pallas kernels, relay_body(): pl.pallas_call(functools.partial(relay_kernel, devices), out_shape=(jax.S...  38.9 us
    unnamed x15, local copies, waits for them, and re-layouts  9.13 us

commit v1 on v0

--- a/solution.py
+++ b/solution.py
@@ -169,44 +169,68 @@
 
 LANES = 128
 RIM = 16
+PARTS = 2
 MESH = pl.DeviceIdType.MESH
 
 
-def half_step_tables(tokens):
-    odd = 2 * np.arange(tokens, dtype=np.int64)[:, None] + 1
+def half_step_tables(tokens, devices):
+    half = tokens // 2
+    odd = 2 * np.arange(half, dtype=np.int64)[:, None] + 1
     turns = (odd * np.arange(tokens, dtype=np.int64)[None, :]) % (4 * tokens)
     angles = turns * (2.0 * np.pi / (4 * tokens))
-    forward = np.concatenate([np.cos(angles), np.sin(angles)], axis=0)
-    pairs = []
-    for table in (forward, forward.T):
-        high = table.astype(jnp.bfloat16)
-        low = (table - high.astype(np.float64)).astype(jnp.bfloat16)
-        pairs += [high, low]
-    return pairs
+    part = half // PARTS
+    share = tokens // devices // 2
+    forward, inverse = [], []
+    for parity in range(2):
+        cosines, sines = np.cos(angles[:, parity::2]), np.sin(angles[:, parity::2])
+        for first in range(0, half, part):
+            forward.append(pair(np.concatenate([cosines[first : first + part], sines[first : first + part]])))
+        back = np.concatenate([cosines, sines]).T
+        back = np.concatenate([back, np.zeros((RIM, 2 * half))])
+        for first in range(0, half, share):
+            inverse.append(pair(back[first : first + share + RIM]))
+    return (
+        np.stack(forward).reshape(2, PARTS, 4 * part, half),
+        np.stack(inverse).reshape(2, devices, 2 * (share + RIM), 2 * half),
+    )
+
+
+def pair(table):
+    high = table.astype(jnp.bfloat16)
+    low = (table - high.astype(np.float64)).astype(jnp.bfloat16)
+    return np.concatenate([high, low])
 
 
 def relay_kernel(
-    devices, go, vb, kg, qg, sw, lf, fwd_hi_hbm, fwd_lo_hbm, inv_hi_hbm, inv_lo_hbm,
+    devices, go_hbm, vb_hbm, kg_hbm, qg_hbm, sw, lf, fwd_hbm, inv_hbm,
     passed, fold_out,
-    conv_src, gated_src, conv_all, filt_all, gated_all, fwd_hi, fwd_lo, inv_hi, inv_lo,
+    go, vb, kg, qg,
+    conv_src, gated_src, conv_all, filt_all, gated_all, fwd, inv, mixed,
     spec_conv, spec_other, packed, back_src, fold_src, back_got, fold_got, key_got, weight_got,
-    table_sem, own_sem, send_sem, recv_sem, back_send, back_recv, side_send, side_recv,
+    load_sem, own_sem, send_sem, recv_sem, back_send, back_recv, side_send, side_recv,
 ):
-    rows = go.shape[1]
+    rows = go.shape[0]
     tokens = rows * devices
+    half = tokens // 2
+    share = rows // 2
     pipe = lax.axis_index("pipe")
     me = lax.axis_index("seq")
     other = 1 - pipe
-
-    tables = [
-        pltpu.make_async_copy(source, target, table_sem.at[i])
-        for i, (source, target) in enumerate(
-            ((fwd_hi_hbm, fwd_hi), (fwd_lo_hbm, fwd_lo), (inv_hi_hbm, inv_hi), (inv_lo_hbm, inv_lo))
-        )
-    ]
+    far_first = sorted(range(1, devices), key=lambda d: (abs(2 * d - devices), d))
+
+    loads = []
+    for i, (source, target) in enumerate(
+        ((go_hbm.at[0], go), (qg_hbm.at[0], qg), (kg_hbm.at[0], kg), (vb_hbm.at[0], vb), (fwd_hbm, fwd), (inv_hbm, inv))
+    ):
+        copy = pltpu.make_async_copy(source, target, load_sem.at[i])
+        copy.start()
+        loads.append(copy)
 
     def peer(distance):
         return lax.rem(me + distance, devices)
+
+    def behind(distance):
+        return lax.rem(me + devices - distance, devices)
 
     barrier = pltpu.get_barrier_semaphore()
     for distance in range(devices):
@@ -217,26 +241,20 @@
         pl.semaphore_signal(
             barrier, inc=1, device_id={"pipe": other, "seq": peer(distance)}, device_id_type=MESH
         )
-    for copy in tables:
-        copy.start()
-    conv_src[...] = (qg[0].astype(jnp.float32) * go[0].astype(jnp.float32)).astype(jnp.bfloat16)
-    gated_src[...] = (kg[0].astype(jnp.float32) * vb[0].astype(jnp.float32)).astype(jnp.bfloat16)
-    back_src[pl.ds(tokens, RIM), :] = jnp.zeros((RIM, LANES), jnp.bfloat16)
+    loads[0].wait()
+    loads[1].wait()
+    conv_src[...] = (qg[...].astype(jnp.float32) * go[...].astype(jnp.float32)).astype(jnp.bfloat16)
     pl.semaphore_wait(barrier, 2 * devices - 1)
 
     def lanes_of(device):
         return pl.ds(pl.multiple_of(device * LANES, LANES), LANES)
 
-    def rows_of(device, extra=0):
-        return pl.ds(pl.multiple_of(device * rows, rows), rows + extra)
+    def rows_of(device):
+        return pl.ds(pl.multiple_of(device * rows, rows), rows)
 
     def scatter(kind, source, target):
-        own = pltpu.make_async_copy(
-            source.at[:, lanes_of(me)], target.at[rows_of(me)], own_sem.at[kind]
-        )
-        own.start()
         copies = []
-        for distance in range(1, devices):
+        for distance in far_first:
             copy = pltpu.make_async_remote_copy(
                 src_ref=source.at[:, lanes_of(peer(distance))],
                 dst_ref=target.at[rows_of(me)],
@@ -247,6 +265,10 @@
             )
             copy.start()
             copies.append(copy)
+        own = pltpu.make_async_copy(
+            source.at[:, lanes_of(me)], target.at[rows_of(me)], own_sem.at[kind]
+        )
+        own.start()
         return own, copies
 
     def landed(group):
@@ -257,13 +279,16 @@
 
     filt_group = scatter(0, lf.at[0], filt_all)
     conv_group = scatter(1, conv_src, conv_all)
+    loads[2].wait()
+    loads[3].wait()
+    gated_src[...] = (kg[...].astype(jnp.float32) * vb[...].astype(jnp.float32)).astype(jnp.bfloat16)
     gated_group = scatter(2, gated_src, gated_all)
     side = []
     for i, (source, target, at) in enumerate(
         (
-            (kg.at[0], key_got.at[pl.ds(0, rows)], me),
-            (kg.at[0, pl.ds(0, RIM)], key_got.at[pl.ds(rows, RIM)], peer(devices - 1)),
-            (sw.at[0], weight_got, me),
+            (kg, key_got.at[pl.ds(0, rows)], me),
+            (kg.at[pl.ds(0, RIM)], key_got.at[pl.ds(rows, RIM)], behind(1)),
+            (sw, weight_got, me),
         )
     ):
         copy = pltpu.make_async_remote_copy(
@@ -273,57 +298,67 @@
         copy.start()
         side.append(copy)
 
-    step = tokens // 2
+    part = half // PARTS
 
     def transform(signal, target):
-        @pl.loop(0, 2 * tokens // step)
-        def _(part):
-            at = pl.ds(pl.multiple_of(part * step, step), step)
-            values = signal[...]
-            target[at, :] = jnp.dot(
-                fwd_hi[at, :], values, preferred_element_type=jnp.float32
-            ) + jnp.dot(fwd_lo[at, :], values, preferred_element_type=jnp.float32)
-
-    def pack(at, value):
+        mixed[pl.ds(0, tokens), :] = signal[...].astype(jnp.float32)
+        evens = mixed[pl.ds(0, half, stride=2), :].astype(jnp.bfloat16)
+        odds = mixed[pl.ds(1, half, stride=2), :].astype(jnp.bfloat16)
+        for i in range(PARTS):
+            even = jnp.dot(fwd[0, i], evens, preferred_element_type=jnp.float32)
+            even = even[: 2 * part] + even[2 * part :]
+            odd = jnp.dot(fwd[1, i], odds, preferred_element_type=jnp.float32)
+            odd = odd[: 2 * part] + odd[2 * part :]
+            at = pl.ds(i * part, part)
+            target[0, at, :] = even[:part] + odd[:part]
+            target[1, at, :] = even[:part] - odd[:part]
+            target[2, at, :] = odd[part:] + even[part:]
+            target[3, at, :] = odd[part:] - even[part:]
+
+    def pack(parity, at, value):
         high = value.astype(jnp.bfloat16)
-        packed[at, pl.ds(0, LANES)] = high
-        packed[at, pl.ds(LANES, LANES)] = (value - high.astype(jnp.float32)).astype(jnp.bfloat16)
-
-    def correlate(target):
-        chunk = rows
-
-        @pl.loop(0, tokens // chunk)
-        def _(part):
-            top = pl.ds(pl.multiple_of(part * chunk, chunk), chunk)
-            low = pl.ds(pl.multiple_of(tokens + part * chunk, chunk), chunk)
-            conv_cos, conv_sin = spec_conv[top, :], spec_conv[low, :]
-            other_cos, other_sin = spec_other[top, :], spec_other[low, :]
+        packed[parity, at, pl.ds(0, LANES)] = high
+        packed[parity, at, pl.ds(LANES, LANES)] = (value - high.astype(jnp.float32)).astype(jnp.bfloat16)
+
+    def multiply():
+        chunk = LANES
+
+        @pl.loop(0, half // chunk)
+        def _(step):
+            at = pl.ds(pl.multiple_of(step * chunk, chunk), chunk)
+            low = pl.ds(pl.multiple_of(half + step * chunk, chunk), chunk)
             scale = 1.0 / tokens
-            pack(top, (conv_cos * other_cos + conv_sin * other_sin) * scale)
-            pack(low, (conv_sin * other_cos - conv_cos * other_sin) * scale)
-
-        @pl.loop(0, tokens // chunk)
-        def _(part):
-            at = pl.ds(pl.multiple_of(part * chunk, chunk), chunk)
-            wide = jnp.dot(inv_hi[at, :], packed[...], preferred_element_type=jnp.float32)
-            narrow = jnp.dot(
-                inv_lo[at, :], packed[:, pl.ds(0, LANES)], preferred_element_type=jnp.float32
-            )
-            target[at, :] = (wide[:, :LANES] + wide[:, LANES:] + narrow).astype(jnp.bfloat16)
+            alike, cross = [], []
+            for side_at in range(2):
+                conv_cos, conv_sin = spec_conv[side_at, at, :] * scale, spec_conv[2 + side_at, at, :] * scale
+                other_cos, other_sin = spec_other[side_at, at, :], spec_other[2 + side_at, at, :]
+                alike.append(conv_cos * other_cos + conv_sin * other_sin)
+                cross.append(conv_sin * other_cos - conv_cos * other_sin)
+            pack(0, at, alike[0] + alike[1])
+            pack(0, low, cross[0] - cross[1])
+            pack(1, at, alike[0] - alike[1])
+            pack(1, low, cross[0] + cross[1])
+
+    def invert(block):
+        for parity in range(2):
+            wide = jnp.dot(inv[parity, block], packed[parity], preferred_element_type=jnp.float32)
+            wide = wide[: share + RIM] + wide[share + RIM :]
+            wide = wide[:, :LANES] + wide[:, LANES:]
+            mixed[pl.ds(parity, share + RIM, stride=2), :] = wide
 
     landed(filt_group)
-    tables[0].wait()
-    tables[1].wait()
+    loads[4].wait()
     transform(filt_all, spec_other)
     landed(conv_group)
     transform(conv_all, spec_conv)
-    tables[2].wait()
-    tables[3].wait()
-    correlate(back_src)
+    multiply()
+    loads[5].wait()
     backs = []
-    for distance in range(devices):
+    for distance in far_first + [0]:
+        invert(peer(distance))
+        back_src[distance] = mixed[pl.ds(0, rows + RIM), :].astype(jnp.bfloat16)
         copy = pltpu.make_async_remote_copy(
-            src_ref=back_src.at[rows_of(peer(distance), RIM)],
+            src_ref=back_src.at[distance],
             dst_ref=back_got.at[me],
             send_sem=back_send.at[distance],
             recv_sem=back_recv.at[distance],
@@ -335,13 +370,13 @@
 
     landed(gated_group)
     transform(gated_all, spec_other)
-    correlate(fold_src)
-    own = pltpu.make_async_copy(fold_src.at[rows_of(me)], fold_got.at[me], own_sem.at[3])
-    own.start()
+    multiply()
     folds = []
-    for distance in range(1, devices):
+    for distance in far_first:
+        invert(peer(distance))
+        fold_src[distance] = mixed[pl.ds(0, rows), :].astype(jnp.bfloat16)
         copy = pltpu.make_async_remote_copy(
-            src_ref=fold_src.at[rows_of(peer(distance))],
+            src_ref=fold_src.at[distance],
             dst_ref=fold_got.at[me],
             send_sem=send_sem.at[3, distance],
             recv_sem=recv_sem.at[3, distance],
@@ -350,22 +385,23 @@
         )
         copy.start()
         folds.append(copy)
-
-    for copy in side + backs:
+    invert(me)
+    fold_out[0, :, lanes_of(me)] = mixed[pl.ds(0, rows), :]
+
+    for copy in side:
         copy.wait_recv()
-    for block in range(devices):
-        columns = pl.ds(block * LANES, LANES)
-        value = key_got[:, columns].astype(jnp.float32) * back_got[block].astype(jnp.float32)
+    for copy, distance in zip(backs, far_first + [0]):
+        copy.wait_recv()
+        columns = lanes_of(behind(distance))
+        value = key_got[:, columns].astype(jnp.float32) * back_got[behind(distance)].astype(jnp.float32)
         extent = rows + RIM
-        total = weight_got[pl.ds(0, 1), columns] * value
-        total += weight_got[pl.ds(1, 1), columns] * pltpu.roll(value, extent - 1, 0)
-        total += weight_got[pl.ds(2, 1), columns] * pltpu.roll(value, extent - 2, 0)
+        total = weight_got[0, :, columns] * value
+        total += weight_got[1, :, columns] * pltpu.roll(value, extent - 1, 0)
+        total += weight_got[2, :, columns] * pltpu.roll(value, extent - 2, 0)
         passed[0, :, columns] = total[:rows].astype(jnp.bfloat16)
-    own.wait()
-    for copy in folds:
+    for copy, distance in zip(folds, far_first):
         copy.wait_recv()
-    for block in range(devices):
-        fold_out[0, :, pl.ds(block * LANES, LANES)] = fold_got[block].astype(jnp.float32)
+        fold_out[0, :, lanes_of(behind(distance))] = fold_got[behind(distance)].astype(jnp.float32)
     for copy in filt_group[1] + conv_group[1] + gated_group[1] + side + backs + folds:
         copy.wait_send()
 
@@ -374,9 +410,9 @@
     _, rows, columns = grad_out.shape
     devices = lax.axis_size("seq")
     tokens = rows * devices
-    tables = [jnp.asarray(table) for table in half_step_tables(tokens)]
+    tables = [jnp.asarray(table) for table in half_step_tables(tokens, devices)]
     vmem = pl.BlockSpec(memory_space=pltpu.VMEM)
-    anywhere = pl.BlockSpec(memory_space=pl.ANY)
+    anywhere = pl.BlockSpec(memory_space=pltpu.HBM)
     half, full = jnp.bfloat16, jnp.float32
     return pl.pallas_call(
         functools.partial(relay_kernel, devices),
@@ -384,29 +420,25 @@
             jax.ShapeDtypeStruct((1, rows, columns), half),
             jax.ShapeDtypeStruct((1, rows, columns), full),
         ),
-        in_specs=[vmem] * 6 + [anywhere] * 4,
+        in_specs=[anywhere] * 8,
         out_specs=(vmem, vmem),
-        scratch_shapes=[
-            pltpu.VMEM((rows, columns), half),
-            pltpu.VMEM((rows, columns), half),
-            pltpu.VMEM((tokens, LANES), half),
-            pltpu.VMEM((tokens, LANES), half),
-            pltpu.VMEM((tokens, LANES), half),
-            pltpu.VMEM((2 * tokens, tokens), half),
-            pltpu.VMEM((2 * tokens, tokens), half),
-            pltpu.VMEM((tokens, 2 * tokens), half),
-            pltpu.VMEM((tokens, 2 * tokens), half),
-            pltpu.VMEM((2 * tokens, LANES), full),
-            pltpu.VMEM((2 * tokens, LANES), full),
-            pltpu.VMEM((2 * tokens, 2 * LANES), half),
-            pltpu.VMEM((tokens + RIM, LANES), half),
-            pltpu.VMEM((tokens, LANES), half),
+        scratch_shapes=[pltpu.VMEM((rows, columns), half)] * 6
+        + [pltpu.VMEM((tokens, LANES), half)] * 3
+        + [
+            pltpu.VMEM(tables[0].shape, half),
+            pltpu.VMEM(tables[1].shape, half),
+            pltpu.VMEM((tokens + 2 * RIM, LANES), full),
+            pltpu.VMEM((4, tokens // 2, LANES), full),
+            pltpu.VMEM((4, tokens // 2, LANES), full),
+            pltpu.VMEM((2, tokens, 2 * LANES), half),
+            pltpu.VMEM((devices, rows + RIM, LANES), half),
+            pltpu.VMEM((devices, rows, LANES), half),
             pltpu.VMEM((devices, rows + RIM, LANES), half),
             pltpu.VMEM((devices, rows, LANES), half),
             pltpu.VMEM((rows + RIM, columns), half),
-            pltpu.VMEM((3, columns), full),
-            pltpu.SemaphoreType.DMA((4,)),
-            pltpu.SemaphoreType.DMA((4,)),
+            pltpu.VMEM((3, 1, columns), full),
+            pltpu.SemaphoreType.DMA((6,)),
+            pltpu.SemaphoreType.DMA((3,)),
             pltpu.SemaphoreType.DMA((4, devices)),
             pltpu.SemaphoreType.DMA((4, devices)),
             pltpu.SemaphoreType.DMA((devices,)),
@@ -415,12 +447,15 @@
             pltpu.SemaphoreType.DMA((3,)),
         ],
         compiler_params=pltpu.CompilerParams(
-            collective_id=0, has_side_effects=True, vmem_limit_bytes=44 * 2**20
+            collective_id=0, has_side_effects=True, vmem_limit_bytes=63 * 2**20
         ),
         cost_estimate=pl.CostEstimate(
-            flops=28 * tokens * tokens * LANES, bytes_accessed=16 * tokens * tokens, transcendentals=0
+            flops=16 * tokens * tokens * LANES, bytes_accessed=10 * tokens * tokens, transcendentals=0
         ),
-    )(grad_out, value_branch, key_gate, query_gate, short_weights, long_filters, *tables)
+    )(
+        grad_out, value_branch, key_gate, query_gate,
+        jnp.transpose(short_weights, (1, 0, 2)), long_filters, *tables,
+    )
 
 
 def solution(mesh):
@@ -441,7 +476,8 @@
             and devices > 1
             and channels == mesh.shape["chan"] * devices * LANES
             and tokens <= 1024
-            and tokens % (devices * RIM) == 0
+            and tokens % (2 * devices * RIM) == 0
+            and tokens % (2 * LANES) == 0
         )
         return jax.shard_map(
             relay_body if fits else spread_body,

time: 49 us -> 40.4 us (0.82)
  local copies, waits for them, and re-layouts: 9.13 us -> 3.54 us
  Pallas kernels: 38.9 us -> 36 us
    unnamed x15 -> x2, local copies, waits for them, and re-layouts: 9.13 us -> 3.54 us
    pallas_call x1, Pallas kernels: 38.9 us -> 36 us  [relay_body(): pl.pallas_call(functools.partial(relay_kernel, devices), out_shape=(jax.S...]
where the time goes in v1:
time: 40.4 us; the launch traced here: 40.2 us
  Pallas kernels  36 us (89%)
  local copies, waits for them, and re-layouts  3.54 us (9%)
  between operations  0.64 us (2%)
    pallas_call x1, Pallas kernels, relay_body(): pl.pallas_call(functools.partial(relay_kernel, devices), out_shape=(jax.S...  36 us
    unnamed x2, local copies, waits for them, and re-layouts  3.54 us

profile of v1, /device:TPU:0, one launch (start us, length us, event | category | flops | bytes accessed | tf_op | source)
XLA Modules:
  0.0 40.2 jit_solution(3530863735927091233)
XLA Ops:
  0.6 36.0 %shard_map.95 = (bf16[1,256,512]{2,1,0:T(8,128)(2,1)}, f32[1,256,512]{2,1,0:T(8,128)}) custom-call(bf16[1,256,512]{2,1,0:T(8,128)(2,1)} %go_hbm.1, bf16[1,256,512]{2,1,0:T(8,128)(2,1)} %vb_hbm.1, bf16[1,256,512]{2,1,0:T(8,128)(2,1)} %kg_hbm.1, bf16[1,256,512]{2,1,0:T(8,128)(2,1)} %qg_hbm.1, f32[3,1,512]{2,1,0:T(1,128)} %bitcast.1, bf16[1,256,512]{2,1,0:T(8,128)(2,1)} %lf.1, ...), custom_call_target="tpu_custom_call" | custom-call | flops 2147483648 | bytes 10485760 | tf_op jit(solution)/shard_map/pallas_call | solution.py:417
  36.6 1.7 %copy.12 = bf16[1,256,512]{2,1,0:T(8,128)(2,1)} copy(bf16[1,256,512]{2,1,0:T(8,128)(2,1)} %get-tuple-element.4) | data formatting | bytes 524288
  38.3 1.9 %copy.13 = f32[1,256,512]{2,1,0:T(8,128)} copy(f32[1,256,512]{2,1,0:T(8,128)} %get-tuple-element.5) | data formatting | bytes 1048576

commit v2 on v1

--- a/solution.py
+++ b/solution.py
@@ -205,9 +205,9 @@
     devices, go_hbm, vb_hbm, kg_hbm, qg_hbm, sw, lf, fwd_hbm, inv_hbm,
     passed, fold_out,
     go, vb, kg, qg,
-    conv_src, gated_src, conv_all, filt_all, gated_all, fwd, inv, mixed,
+    conv_src, gated_src, filt_src, conv_all, filt_all, gated_all, fwd, inv, mixed,
     spec_conv, spec_other, packed, back_src, fold_src, back_got, fold_got, key_got, weight_got,
-    load_sem, own_sem, send_sem, recv_sem, back_send, back_recv, side_send, side_recv,
+    load_sem, filt_sem, own_sem, send_sem, recv_sem, back_send, back_recv, side_send, side_recv,
 ):
     rows = go.shape[0]
     tokens = rows * devices
@@ -226,6 +226,20 @@
         copy.start()
         loads.append(copy)
 
+    filt_loads = []
+    for block in range(devices):
+        copy = pltpu.make_async_copy(
+            lf.at[0, :, pl.ds(block * LANES, LANES)], filt_src.at[block], filt_sem.at[block]
+        )
+        copy.start()
+        filt_loads.append(copy)
+
+    def gate(left, right, target):
+        for block in range(devices):
+            columns = pl.ds(block * LANES, LANES)
+            value = left[:, columns].astype(jnp.float32) * right[:, columns].astype(jnp.float32)
+            target[block] = value.astype(jnp.bfloat16)
+
     def peer(distance):
         return lax.rem(me + distance, devices)
 
@@ -243,7 +257,9 @@
         )
     loads[0].wait()
     loads[1].wait()
-    conv_src[...] = (qg[...].astype(jnp.float32) * go[...].astype(jnp.float32)).astype(jnp.bfloat16)
+    gate(qg, go, conv_src)
+    for copy in filt_loads:
+        copy.wait()
     pl.semaphore_wait(barrier, 2 * devices - 1)
 
     def lanes_of(device):
@@ -256,7 +272,7 @@
         copies = []
         for distance in far_first:
             copy = pltpu.make_async_remote_copy(
-                src_ref=source.at[:, lanes_of(peer(distance))],
+                src_ref=source.at[peer(distance)],
                 dst_ref=target.at[rows_of(me)],
                 send_sem=send_sem.at[kind, distance],
                 recv_sem=recv_sem.at[kind, distance],
@@ -266,7 +282,7 @@
             copy.start()
             copies.append(copy)
         own = pltpu.make_async_copy(
-            source.at[:, lanes_of(me)], target.at[rows_of(me)], own_sem.at[kind]
+            source.at[me], target.at[rows_of(me)], own_sem.at[kind]
         )
         own.start()
         return own, copies
@@ -277,12 +293,11 @@
         for copy in copies:
             copy.wait_recv()
 
-    filt_group = scatter(0, lf.at[0], filt_all)
+    filt_group = scatter(0, filt_src, filt_all)
     conv_group = scatter(1, conv_src, conv_all)
     loads[2].wait()
     loads[3].wait()
-    gated_src[...] = (kg[...].astype(jnp.float32) * vb[...].astype(jnp.float32)).astype(jnp.bfloat16)
-    gated_group = scatter(2, gated_src, gated_all)
+    gate(kg, vb, gated_src)
     side = []
     for i, (source, target, at) in enumerate(
         (
@@ -298,6 +313,9 @@
         copy.start()
         side.append(copy)
 
+    for copy in filt_group[1]:
+        copy.wait_send()
+    gated_group = scatter(2, gated_src, gated_all)
     part = half // PARTS
 
     def transform(signal, target):
@@ -402,7 +420,7 @@
     for copy, distance in zip(folds, far_first):
         copy.wait_recv()
         fold_out[0, :, lanes_of(behind(distance))] = fold_got[behind(distance)].astype(jnp.float32)
-    for copy in filt_group[1] + conv_group[1] + gated_group[1] + side + backs + folds:
+    for copy in conv_group[1] + gated_group[1] + side + backs + folds:
         copy.wait_send()
 
 
@@ -417,12 +435,13 @@
     return pl.pallas_call(
         functools.partial(relay_kernel, devices),
         out_shape=(
-            jax.ShapeDtypeStruct((1, rows, columns), half),
-            jax.ShapeDtypeStruct((1, rows, columns), full),
+            pltpu.VMEM((1, rows, columns), half),
+            pltpu.VMEM((1, rows, columns), full),
         ),
         in_specs=[anywhere] * 8,
         out_specs=(vmem, vmem),
-        scratch_shapes=[pltpu.VMEM((rows, columns), half)] * 6
+        scratch_shapes=[pltpu.VMEM((rows, columns), half)] * 4
+        + [pltpu.VMEM((devices, rows, LANES), half)] * 3
         + [pltpu.VMEM((tokens, LANES), half)] * 3
         + [
             pltpu.VMEM(tables[0].shape, half),
@@ -438,6 +457,7 @@
             pltpu.VMEM((rows + RIM, columns), half),
             pltpu.VMEM((3, 1, columns), full),
             pltpu.SemaphoreType.DMA((6,)),
+            pltpu.SemaphoreType.DMA((devices,)),
             pltpu.SemaphoreType.DMA((3,)),
             pltpu.SemaphoreType.DMA((4, devices)),
             pltpu.SemaphoreType.DMA((4, devices)),
@@ -447,7 +467,7 @@
             pltpu.SemaphoreType.DMA((3,)),
         ],
         compiler_params=pltpu.CompilerParams(
-            collective_id=0, has_side_effects=True, vmem_limit_bytes=63 * 2**20
+            collective_id=0, has_side_effects=True, vmem_limit_bytes=62 * 2**20
         ),
         cost_estimate=pl.CostEstimate(
             flops=16 * tokens * tokens * LANES, bytes_accessed=10 * tokens * tokens, transcendentals=0

time: 40.4 us -> 39.5 us (0.978)
  local copies, waits for them, and re-layouts: 3.54 us -> 1.5 us
  Pallas kernels: 36 us -> 37.2 us
    unnamed x2, local copies, waits for them, and re-layouts: 3.54 us -> 1.5 us
    pallas_call x1, Pallas kernels: 36 us -> 37.2 us  [relay_body(): pl.pallas_call(functools.partial(relay_kernel, devices), out_shape=(pltpu...]
where the time goes in v2:
time: 39.5 us; the launch traced here: 39.4 us
  Pallas kernels  37.2 us (94%)
  local copies, waits for them, and re-layouts  1.5 us (4%)
  between operations  0.64 us (2%)
    pallas_call x1, Pallas kernels, relay_body(): pl.pallas_call(functools.partial(relay_kernel, devices), out_shape=(pltpu...  37.2 us
    unnamed x2, local copies, waits for them, and re-layouts  1.5 us

profile of v2, /device:TPU:0, one launch (start us, length us, event | category | flops | bytes accessed | tf_op | source)
XLA Modules:
  0.0 39.4 jit_solution(5569327107700558036)
XLA Ops:
  0.6 37.2 %shard_map.95 = (bf16[1,256,512]{2,1,0:T(8,128)(2,1)S(1)}, f32[1,256,512]{2,1,0:T(8,128)S(1)}) custom-call(bf16[1,256,512]{2,1,0:T(8,128)(2,1)} %go_hbm.1, bf16[1,256,512]{2,1,0:T(8,128)(2,1)} %vb_hbm.1, bf16[1,256,512]{2,1,0:T(8,128)(2,1)} %kg_hbm.1, bf16[1,256,512]{2,1,0:T(8,128)(2,1)} %qg_hbm.1, f32[3,1,512]{2,1,0:T(1,128)} %bitcast.1, ...), custom_call_target="tpu_custom_call" | custom-call | flops 2147483648 | bytes 10485760 | tf_op jit(solution)/shard_map/pallas_call | solution.py:435
  37.9 0.7 %copy.12 = bf16[1,256,512]{2,1,0:T(8,128)(2,1)} copy(bf16[1,256,512]{2,1,0:T(8,128)(2,1)S(1)} %get-tuple-element.2) | data formatting | bytes 524288
  38.6 0.8 %copy.13 = f32[1,256,512]{2,1,0:T(8,128)} copy(f32[1,256,512]{2,1,0:T(8,128)S(1)} %get-tuple-element.3) | data formatting | bytes 1048576

commit v3 on v2

--- a/solution.py
+++ b/solution.py
@@ -205,8 +205,8 @@
     devices, go_hbm, vb_hbm, kg_hbm, qg_hbm, sw, lf, fwd_hbm, inv_hbm,
     passed, fold_out,
     go, vb, kg, qg,
-    conv_src, gated_src, filt_src, conv_all, filt_all, gated_all, fwd, inv, mixed,
-    spec_conv, spec_other, packed, back_src, fold_src, back_got, fold_got, key_got, weight_got,
+    conv_src, gated_src, filt_src, both_all, gated_all, fwd, inv, mixed, woven,
+    spec_both, spec_gated, packed, back_src, fold_src, back_got, fold_got, key_got, weight_got,
     load_sem, filt_sem, own_sem, send_sem, recv_sem, back_send, back_recv, side_send, side_recv,
 ):
     rows = go.shape[0]
@@ -268,12 +268,16 @@
     def rows_of(device):
         return pl.ds(pl.multiple_of(device * rows, rows), rows)
 
-    def scatter(kind, source, target):
+    first, second = pl.ds(0, LANES), pl.ds(LANES, LANES)
+
+    def scatter(kind, source, target, columns, before=()):
         copies = []
-        for distance in far_first:
+        for i, distance in enumerate(far_first):
+            if before:
+                before[i].wait_send()
             copy = pltpu.make_async_remote_copy(
                 src_ref=source.at[peer(distance)],
-                dst_ref=target.at[rows_of(me)],
+                dst_ref=target.at[rows_of(me), columns],
                 send_sem=send_sem.at[kind, distance],
                 recv_sem=recv_sem.at[kind, distance],
                 device_id={"pipe": pipe, "seq": peer(distance)},
@@ -282,7 +286,7 @@
             copy.start()
             copies.append(copy)
         own = pltpu.make_async_copy(
-            source.at[me], target.at[rows_of(me)], own_sem.at[kind]
+            source.at[me], target.at[rows_of(me), columns], own_sem.at[kind]
         )
         own.start()
         return own, copies
@@ -293,8 +297,8 @@
         for copy in copies:
             copy.wait_recv()
 
-    filt_group = scatter(0, filt_src, filt_all)
-    conv_group = scatter(1, conv_src, conv_all)
+    filt_group = scatter(0, filt_src, both_all, first)
+    conv_group = scatter(1, conv_src, both_all, second)
     loads[2].wait()
     loads[3].wait()
     gate(kg, vb, gated_src)
@@ -313,15 +317,17 @@
         copy.start()
         side.append(copy)
 
-    for copy in filt_group[1]:
-        copy.wait_send()
-    gated_group = scatter(2, gated_src, gated_all)
+    gated_group = scatter(2, gated_src, gated_all, first, filt_group[1])
     part = half // PARTS
 
     def transform(signal, target):
-        mixed[pl.ds(0, tokens), :] = signal[...].astype(jnp.float32)
-        evens = mixed[pl.ds(0, half, stride=2), :].astype(jnp.bfloat16)
-        odds = mixed[pl.ds(1, half, stride=2), :].astype(jnp.bfloat16)
+        width = signal.shape[1]
+        evens, odds = [], []
+        for at in range(0, width, LANES):
+            mixed[...] = signal[:, pl.ds(at, LANES)].astype(jnp.float32)
+            evens.append(mixed[pl.ds(0, half, stride=2), :].astype(jnp.bfloat16))
+            odds.append(mixed[pl.ds(1, half, stride=2), :].astype(jnp.bfloat16))
+        evens, odds = jnp.concatenate(evens, axis=1), jnp.concatenate(odds, axis=1)
         for i in range(PARTS):
             even = jnp.dot(fwd[0, i], evens, preferred_element_type=jnp.float32)
             even = even[: 2 * part] + even[2 * part :]
@@ -333,13 +339,13 @@
             target[2, at, :] = odd[part:] + even[part:]
             target[3, at, :] = odd[part:] - even[part:]
 
-    def pack(parity, at, value):
+    def pack(kind, parity, at, value):
         high = value.astype(jnp.bfloat16)
-        packed[parity, at, pl.ds(0, LANES)] = high
-        packed[parity, at, pl.ds(LANES, LANES)] = (value - high.astype(jnp.float32)).astype(jnp.bfloat16)
-
-    def multiply():
-        chunk = LANES
+        packed[kind, parity, at, first] = high
+        packed[kind, parity, at, second] = (value - high.astype(jnp.float32)).astype(jnp.bfloat16)
+
+    def multiply(kind, spec_other):
+        chunk = 64
 
         @pl.loop(0, half // chunk)
         def _(step):
@@ -347,34 +353,27 @@
             low = pl.ds(pl.multiple_of(half + step * chunk, chunk), chunk)
             scale = 1.0 / tokens
             alike, cross = [], []
-            for side_at in range(2):
-                conv_cos, conv_sin = spec_conv[side_at, at, :] * scale, spec_conv[2 + side_at, at, :] * scale
-                other_cos, other_sin = spec_other[side_at, at, :], spec_other[2 + side_at, at, :]
+            for mirror in range(2):
+                conv_cos = spec_both[mirror, at, second] * scale
+                conv_sin = spec_both[2 + mirror, at, second] * scale
+                other_cos, other_sin = spec_other[mirror, at, first], spec_other[2 + mirror, at, first]
                 alike.append(conv_cos * other_cos + conv_sin * other_sin)
                 cross.append(conv_sin * other_cos - conv_cos * other_sin)
-            pack(0, at, alike[0] + alike[1])
-            pack(0, low, cross[0] - cross[1])
-            pack(1, at, alike[0] - alike[1])
-            pack(1, low, cross[0] + cross[1])
-
-    def invert(block):
+            pack(kind, 0, at, alike[0] + alike[1])
+            pack(kind, 0, low, cross[0] - cross[1])
+            pack(kind, 1, at, alike[0] - alike[1])
+            pack(kind, 1, low, cross[0] + cross[1])
+
+    def invert(kind, block):
         for parity in range(2):
-            wide = jnp.dot(inv[parity, block], packed[parity], preferred_element_type=jnp.float32)
+            wide = jnp.dot(inv[parity, block], packed[kind, parity], preferred_element_type=jnp.float32)
             wide = wide[: share + RIM] + wide[share + RIM :]
             wide = wide[:, :LANES] + wide[:, LANES:]
-            mixed[pl.ds(parity, share + RIM, stride=2), :] = wide
-
-    landed(filt_group)
-    loads[4].wait()
-    transform(filt_all, spec_other)
-    landed(conv_group)
-    transform(conv_all, spec_conv)
-    multiply()
-    loads[5].wait()
-    backs = []
-    for distance in far_first + [0]:
-        invert(peer(distance))
-        back_src[distance] = mixed[pl.ds(0, rows + RIM), :].astype(jnp.bfloat16)
+            woven[pl.ds(parity, share + RIM, stride=2), :] = wide
+
+    def send_back(distance):
+        invert(0, peer(distance))
+        back_src[distance] = woven[pl.ds(0, rows + RIM), :].astype(jnp.bfloat16)
         copy = pltpu.make_async_remote_copy(
             src_ref=back_src.at[distance],
             dst_ref=back_got.at[me],
@@ -384,15 +383,11 @@
             device_id_type=MESH,
         )
         copy.start()
-        backs.append(copy)
-
-    landed(gated_group)
-    transform(gated_all, spec_other)
-    multiply()
-    folds = []
-    for distance in far_first:
-        invert(peer(distance))
-        fold_src[distance] = mixed[pl.ds(0, rows), :].astype(jnp.bfloat16)
+        return copy
+
+    def send_fold(distance):
+        invert(1, peer(distance))
+        fold_src[distance] = woven[pl.ds(0, rows), :].astype(jnp.bfloat16)
         copy = pltpu.make_async_remote_copy(
             src_ref=fold_src.at[distance],
             dst_ref=fold_got.at[me],
@@ -402,9 +397,22 @@
             device_id_type=MESH,
         )
         copy.start()
-        folds.append(copy)
-    invert(me)
-    fold_out[0, :, lanes_of(me)] = mixed[pl.ds(0, rows), :]
+        return copy
+
+    loads[4].wait()
+    landed(filt_group)
+    landed(conv_group)
+    transform(both_all, spec_both)
+    multiply(0, spec_both)
+    loads[5].wait()
+    backs = [send_back(distance) for distance in far_first]
+    landed(gated_group)
+    transform(gated_all, spec_gated)
+    multiply(1, spec_gated)
+    folds = [send_fold(distance) for distance in far_first]
+    backs.append(send_back(0))
+    invert(1, me)
+    fold_out[0, :, lanes_of(me)] = woven[pl.ds(0, rows), :]
 
     for copy in side:
         copy.wait_recv()
@@ -442,14 +450,16 @@
         out_specs=(vmem, vmem),
         scratch_shapes=[pltpu.VMEM((rows, columns), half)] * 4
         + [pltpu.VMEM((devices, rows, LANES), half)] * 3
-        + [pltpu.VMEM((tokens, LANES), half)] * 3
         + [
+            pltpu.VMEM((tokens, 2 * LANES), half),
+            pltpu.VMEM((tokens, LANES), half),
             pltpu.VMEM(tables[0].shape, half),
             pltpu.VMEM(tables[1].shape, half),
-            pltpu.VMEM((tokens + 2 * RIM, LANES), full),
+            pltpu.VMEM((tokens, LANES), full),
+            pltpu.VMEM((rows + 2 * RIM, LANES), full),
+            pltpu.VMEM((4, tokens // 2, 2 * LANES), full),
             pltpu.VMEM((4, tokens // 2, LANES), full),
-            pltpu.VMEM((4, tokens // 2, LANES), full),
-            pltpu.VMEM((2, tokens, 2 * LANES), half),
+            pltpu.VMEM((2, 2, tokens, 2 * LANES), half),
             pltpu.VMEM((devices, rows + RIM, LANES), half),
             pltpu.VMEM((devices, rows, LANES), half),
             pltpu.VMEM((devices, rows + RIM, LANES), half),

time: 39.5 us -> 39.5 us (level)
  no operation moved by 1% of the time
where the time goes in v3:
time: 39.5 us; the launch traced here: 39.4 us
  Pallas kernels  37.2 us (94%)
  local copies, waits for them, and re-layouts  1.5 us (4%)
  between operations  0.64 us (2%)
    pallas_call x1, Pallas kernels, relay_body(): pl.pallas_call(functools.partial(relay_kernel, devices), out_shape=(pltpu...  37.2 us
    unnamed x2, local copies, waits for them, and re-layouts  1.5 us

profile of v3, /device:TPU:0, one launch (start us, length us, event | category | flops | bytes accessed | tf_op | source)
XLA Modules:
  0.0 39.4 jit_solution(8057019624311494403)
XLA Ops:
  0.6 37.2 %shard_map.95 = (bf16[1,256,512]{2,1,0:T(8,128)(2,1)S(1)}, f32[1,256,512]{2,1,0:T(8,128)S(1)}) custom-call(bf16[1,256,512]{2,1,0:T(8,128)(2,1)} %go_hbm.1, bf16[1,256,512]{2,1,0:T(8,128)(2,1)} %vb_hbm.1, bf16[1,256,512]{2,1,0:T(8,128)(2,1)} %kg_hbm.1, bf16[1,256,512]{2,1,0:T(8,128)(2,1)} %qg_hbm.1, f32[3,1,512]{2,1,0:T(1,128)} %bitcast.1, ...), custom_call_target="tpu_custom_call" | custom-call | flops 2147483648 | bytes 10485760 | tf_op jit(solution)/shard_map/pallas_call | solution.py:443
  37.9 0.7 %copy.12 = bf16[1,256,512]{2,1,0:T(8,128)(2,1)} copy(bf16[1,256,512]{2,1,0:T(8,128)(2,1)S(1)} %get-tuple-element.2) | data formatting | bytes 524288
  38.6 0.8 %copy.13 = f32[1,256,512]{2,1,0:T(8,128)} copy(f32[1,256,512]{2,1,0:T(8,128)S(1)} %get-tuple-element.3) | data formatting | bytes 1048576

commit v4 on v3

--- a/solution.py
+++ b/solution.py
@@ -170,6 +170,7 @@
 LANES = 128
 RIM = 16
 PARTS = 2
+SPLIT = 4
 MESH = pl.DeviceIdType.MESH
 
 
@@ -270,11 +271,9 @@
 
     first, second = pl.ds(0, LANES), pl.ds(LANES, LANES)
 
-    def scatter(kind, source, target, columns, before=()):
+    def scatter(kind, source, target, columns):
         copies = []
-        for i, distance in enumerate(far_first):
-            if before:
-                before[i].wait_send()
+        for distance in far_first:
             copy = pltpu.make_async_remote_copy(
                 src_ref=source.at[peer(distance)],
                 dst_ref=target.at[rows_of(me), columns],
@@ -317,7 +316,7 @@
         copy.start()
         side.append(copy)
 
-    gated_group = scatter(2, gated_src, gated_all, first, filt_group[1])
+    gated_group = scatter(2, gated_src, gated_all, first)
     part = half // PARTS
 
     def transform(signal, target):
@@ -428,7 +427,7 @@
     for copy, distance in zip(folds, far_first):
         copy.wait_recv()
         fold_out[0, :, lanes_of(behind(distance))] = fold_got[behind(distance)].astype(jnp.float32)
-    for copy in conv_group[1] + gated_group[1] + side + backs + folds:
+    for copy in filt_group[1] + conv_group[1] + gated_group[1] + side + backs + folds:
         copy.wait_send()
 
 
@@ -440,7 +439,7 @@
     vmem = pl.BlockSpec(memory_space=pltpu.VMEM)
     anywhere = pl.BlockSpec(memory_space=pltpu.HBM)
     half, full = jnp.bfloat16, jnp.float32
-    return pl.pallas_call(
+    passed, fold = pl.pallas_call(
         functools.partial(relay_kernel, devices),
         out_shape=(
             pltpu.VMEM((1, rows, columns), half),
@@ -486,6 +485,30 @@
         grad_out, value_branch, key_gate, query_gate,
         jnp.transpose(short_weights, (1, 0, 2)), long_filters, *tables,
     )
+    return pl.pallas_call(
+        settle_kernel,
+        out_shape=(
+            jax.ShapeDtypeStruct(passed.shape, half),
+            jax.ShapeDtypeStruct(fold.shape, full),
+        ),
+        in_specs=[vmem, vmem],
+        out_specs=(anywhere, anywhere),
+        scratch_shapes=[pltpu.SemaphoreType.DMA((2, SPLIT))],
+        compiler_params=pltpu.CompilerParams(vmem_limit_bytes=16 * 2**20),
+    )(passed, fold)
+
+
+def settle_kernel(passed, fold, passed_out, fold_out, sem):
+    copies = []
+    for i, (source, target) in enumerate(((fold, fold_out), (passed, passed_out))):
+        step = source.shape[1] // SPLIT
+        for j in range(SPLIT):
+            at = pl.ds(j * step, step)
+            copies.append(pltpu.make_async_copy(source.at[:, at], target.at[:, at], sem.at[i, j]))
+    for copy in copies:
+        copy.start()
+    for copy in copies:
+        copy.wait()
 
 
 def solution(mesh):

time: 39.5 us -> 39 us (0.987)
  local copies, waits for them, and re-layouts: 1.5 us -> 0 us
  Pallas kernels: 37.2 us -> 38.2 us
    unnamed x2 -> x0, local copies, waits for them, and re-layouts: 1.5 us -> none
    pallas_call x0 -> x1, Pallas kernels: none -> 0.94 us  [relay_body(): pl.pallas_call(settle_kernel, out_shape=(jax.ShapeDtypeStruct(passed.shap...]
where the time goes in v4:
time: 39 us; the launch traced here: 38.8 us
  Pallas kernels  38.2 us (98%)
  between operations  0.64 us (2%)
    pallas_call x1, Pallas kernels, relay_body(): pl.pallas_call(functools.partial(relay_kernel, devices), out_shape=(pltpu...  37.2 us
    pallas_call x1, Pallas kernels, relay_body(): pl.pallas_call(settle_kernel, out_shape=(jax.ShapeDtypeStruct(passed.shap...  0.94 us

profile of v4, /device:TPU:0, one launch (start us, length us, event | category | flops | bytes accessed | tf_op | source)
XLA Modules:
  0.0 38.8 jit_solution(2427152674280126862)
XLA Ops:
  0.6 37.2 %shard_map.95 = (bf16[1,256,512]{2,1,0:T(8,128)(2,1)S(1)}, f32[1,256,512]{2,1,0:T(8,128)S(1)}) custom-call(bf16[1,256,512]{2,1,0:T(8,128)(2,1)} %go_hbm.1, bf16[1,256,512]{2,1,0:T(8,128)(2,1)} %vb_hbm.1, bf16[1,256,512]{2,1,0:T(8,128)(2,1)} %kg_hbm.1, bf16[1,256,512]{2,1,0:T(8,128)(2,1)} %qg_hbm.1, f32[3,1,512]{2,1,0:T(1,128)} %bitcast.1, ...), custom_call_target="tpu_custom_call" | custom-call | flops 2147483648 | bytes 10485760 | tf_op jit(solution)/shard_map/pallas_call | solution.py:442
  37.9 0.9 %shard_map.96 = (bf16[1,256,512]{2,1,0:T(8,128)(2,1)}, f32[1,256,512]{2,1,0:T(8,128)}) custom-call(bf16[1,256,512]{2,1,0:T(8,128)(2,1)S(1)} %get-tuple-element.4.passed, f32[1,256,512]{2,1,0:T(8,128)S(1)} %get-tuple-element.5.fold), custom_call_target="tpu_custom_call" | custom-call | tf_op jit(solution)/shard_map/pallas_call | solution.py:488

commit v5 on v4

--- a/solution.py
+++ b/solution.py
@@ -206,9 +206,9 @@
     devices, go_hbm, vb_hbm, kg_hbm, qg_hbm, sw, lf, fwd_hbm, inv_hbm,
     passed, fold_out,
     go, vb, kg, qg,
-    conv_src, gated_src, filt_src, both_all, gated_all, fwd, inv, mixed, woven,
+    conv_src, gated_src, both_all, gated_all, fwd, inv, mixed, woven,
     spec_both, spec_gated, packed, back_src, fold_src, back_got, fold_got, key_got, weight_got,
-    load_sem, filt_sem, own_sem, send_sem, recv_sem, back_send, back_recv, side_send, side_recv,
+    load_sem, own_sem, send_sem, recv_sem, back_send, back_recv, side_send, side_recv,
 ):
     rows = go.shape[0]
     tokens = rows * devices
@@ -219,22 +219,6 @@
     other = 1 - pipe
     far_first = sorted(range(1, devices), key=lambda d: (abs(2 * d - devices), d))
 
-    loads = []
-    for i, (source, target) in enumerate(
-        ((go_hbm.at[0], go), (qg_hbm.at[0], qg), (kg_hbm.at[0], kg), (vb_hbm.at[0], vb), (fwd_hbm, fwd), (inv_hbm, inv))
-    ):
-        copy = pltpu.make_async_copy(source, target, load_sem.at[i])
-        copy.start()
-        loads.append(copy)
-
-    filt_loads = []
-    for block in range(devices):
-        copy = pltpu.make_async_copy(
-            lf.at[0, :, pl.ds(block * LANES, LANES)], filt_src.at[block], filt_sem.at[block]
-        )
-        copy.start()
-        filt_loads.append(copy)
-
     def gate(left, right, target):
         for block in range(devices):
             columns = pl.ds(block * LANES, LANES)
@@ -256,11 +240,14 @@
         pl.semaphore_signal(
             barrier, inc=1, device_id={"pipe": other, "seq": peer(distance)}, device_id_type=MESH
         )
-    loads[0].wait()
-    loads[1].wait()
-    gate(qg, go, conv_src)
-    for copy in filt_loads:
-        copy.wait()
+    loads = []
+    for i, (source, target) in enumerate(
+        ((go_hbm.at[0], go), (qg_hbm.at[0], qg), (kg_hbm.at[0], kg), (vb_hbm.at[0], vb), (fwd_hbm, fwd), (inv_hbm, inv))
+    ):
+        copy = pltpu.make_async_copy(source, target, load_sem.at[i])
+        loads.append(copy)
+    for copy in loads[:4]:
+        copy.start()
     pl.semaphore_wait(barrier, 2 * devices - 1)
 
     def lanes_of(device):
@@ -271,11 +258,11 @@
 
     first, second = pl.ds(0, LANES), pl.ds(LANES, LANES)
 
-    def scatter(kind, source, target, columns):
+    def scatter(kind, pick, target, columns):
         copies = []
         for distance in far_first:
             copy = pltpu.make_async_remote_copy(
-                src_ref=source.at[peer(distance)],
+                src_ref=pick(peer(distance)),
                 dst_ref=target.at[rows_of(me), columns],
                 send_sem=send_sem.at[kind, distance],
                 recv_sem=recv_sem.at[kind, distance],
@@ -285,7 +272,7 @@
             copy.start()
             copies.append(copy)
         own = pltpu.make_async_copy(
-            source.at[me], target.at[rows_of(me), columns], own_sem.at[kind]
+            pick(me), target.at[rows_of(me), columns], own_sem.at[kind]
         )
         own.start()
         return own, copies
@@ -296,8 +283,13 @@
         for copy in copies:
             copy.wait_recv()
 
-    filt_group = scatter(0, filt_src, both_all, first)
-    conv_group = scatter(1, conv_src, both_all, second)
+    filt_group = scatter(0, lambda device: lf.at[0, :, lanes_of(device)], both_all, first)
+    loads[0].wait()
+    loads[1].wait()
+    gate(qg, go, conv_src)
+    conv_group = scatter(1, lambda device: conv_src.at[device], both_all, second)
+    for copy in loads[4:]:
+        copy.start()
     loads[2].wait()
     loads[3].wait()
     gate(kg, vb, gated_src)
@@ -316,7 +308,7 @@
         copy.start()
         side.append(copy)
 
-    gated_group = scatter(2, gated_src, gated_all, first)
+    gated_group = scatter(2, lambda device: gated_src.at[device], gated_all, first)
     part = half // PARTS
 
     def transform(signal, target):
@@ -448,7 +440,7 @@
         in_specs=[anywhere] * 8,
         out_specs=(vmem, vmem),
         scratch_shapes=[pltpu.VMEM((rows, columns), half)] * 4
-        + [pltpu.VMEM((devices, rows, LANES), half)] * 3
+        + [pltpu.VMEM((devices, rows, LANES), half)] * 2
         + [
             pltpu.VMEM((tokens, 2 * LANES), half),
             pltpu.VMEM((tokens, LANES), half),
@@ -466,7 +458,6 @@
             pltpu.VMEM((rows + RIM, columns), half),
             pltpu.VMEM((3, 1, columns), full),
             pltpu.SemaphoreType.DMA((6,)),
-            pltpu.SemaphoreType.DMA((devices,)),
             pltpu.SemaphoreType.DMA((3,)),
             pltpu.SemaphoreType.DMA((4, devices)),
             pltpu.SemaphoreType.DMA((4, devices)),

time: 39 us -> 36.6 us (0.938)
  Pallas kernels: 38.2 us -> 35.9 us
    pallas_call x1, Pallas kernels: 37.2 us -> 34.9 us  [relay_body(): pl.pallas_call(functools.partial(relay_kernel, devices), out_shape=(pltpu...]
where the time goes in v5:
time: 36.6 us; the launch traced here: 36.5 us
  Pallas kernels  35.9 us (98%)
  between operations  0.64 us (2%)
    pallas_call x1, Pallas kernels, relay_body(): pl.pallas_call(functools.partial(relay_kernel, devices), out_shape=(pltpu...  34.9 us
    pallas_call x1, Pallas kernels, relay_body(): pl.pallas_call(settle_kernel, out_shape=(jax.ShapeDtypeStruct(passed.shap...  0.94 us

profile of v5, /device:TPU:0, one launch (start us, length us, event | category | flops | bytes accessed | tf_op | source)
XLA Modules:
  0.0 36.5 jit_solution(245888584389120744)
XLA Ops:
  0.6 34.9 %shard_map.95 = (bf16[1,256,512]{2,1,0:T(8,128)(2,1)S(1)}, f32[1,256,512]{2,1,0:T(8,128)S(1)}) custom-call(bf16[1,256,512]{2,1,0:T(8,128)(2,1)} %go_hbm.1, bf16[1,256,512]{2,1,0:T(8,128)(2,1)} %vb_hbm.1, bf16[1,256,512]{2,1,0:T(8,128)(2,1)} %kg_hbm.1, bf16[1,256,512]{2,1,0:T(8,128)(2,1)} %qg_hbm.1, f32[3,1,512]{2,1,0:T(1,128)} %bitcast.1, ...), custom_call_target="tpu_custom_call" | custom-call | flops 2147483648 | bytes 10485760 | tf_op jit(solution)/shard_map/pallas_call | solution.py:434
  35.6 0.9 %shard_map.96 = (bf16[1,256,512]{2,1,0:T(8,128)(2,1)}, f32[1,256,512]{2,1,0:T(8,128)}) custom-call(bf16[1,256,512]{2,1,0:T(8,128)(2,1)S(1)} %get-tuple-element.4.passed, f32[1,256,512]{2,1,0:T(8,128)S(1)} %get-tuple-element.5.fold), custom_call_target="tpu_custom_call" | custom-call | tf_op jit(solution)/shard_map/pallas_call | solution.py:479

commit v6 on v5

--- a/solution.py
+++ b/solution.py
@@ -208,7 +208,7 @@
     go, vb, kg, qg,
     conv_src, gated_src, both_all, gated_all, fwd, inv, mixed, woven,
     spec_both, spec_gated, packed, back_src, fold_src, back_got, fold_got, key_got, weight_got,
-    load_sem, own_sem, send_sem, recv_sem, back_send, back_recv, side_send, side_recv,
+    load_sem, own_sem, send_sem, recv_sem, back_send, back_recv, side_send, side_recv, late_sem,
 ):
     rows = go.shape[0]
     tokens = rows * devices
@@ -231,15 +231,27 @@
     def behind(distance):
         return lax.rem(me + devices - distance, devices)
 
+    last = devices - 1
+    late = me == last
+
+    def slot_peer(slot):
+        early = lax.rem(me + 1 + slot, last) if slot < last - 1 else last
+        return jnp.where(late, slot, early)
+
+    def greet(semaphore, device_pipe, at):
+        pl.semaphore_signal(
+            semaphore, inc=1, device_id={"pipe": device_pipe, "seq": at}, device_id_type=MESH
+        )
+
     barrier = pltpu.get_barrier_semaphore()
-    for distance in range(devices):
-        if distance:
-            pl.semaphore_signal(
-                barrier, inc=1, device_id={"pipe": pipe, "seq": peer(distance)}, device_id_type=MESH
-            )
-        pl.semaphore_signal(
-            barrier, inc=1, device_id={"pipe": other, "seq": peer(distance)}, device_id_type=MESH
-        )
+    greet(barrier, other, me)
+
+    @pl.when(jnp.logical_not(late))
+    def _():
+        for slot in range(last):
+            greet(barrier, pipe, slot_peer(slot))
+            greet(barrier, other, slot_peer(slot))
+
     loads = []
     for i, (source, target) in enumerate(
         ((go_hbm.at[0], go), (qg_hbm.at[0], qg), (kg_hbm.at[0], kg), (vb_hbm.at[0], vb), (fwd_hbm, fwd), (inv_hbm, inv))
@@ -248,7 +260,13 @@
         loads.append(copy)
     for copy in loads[:4]:
         copy.start()
-    pl.semaphore_wait(barrier, 2 * devices - 1)
+    pl.semaphore_wait(barrier, jnp.where(late, 2 * devices - 1, 2 * last - 1))
+
+    @pl.when(late)
+    def _():
+        for slot in range(last):
+            greet(late_sem, pipe, slot_peer(slot))
+            greet(late_sem, other, slot_peer(slot))
 
     def lanes_of(device):
         return pl.ds(pl.multiple_of(device * LANES, LANES), LANES)
@@ -259,28 +277,32 @@
     first, second = pl.ds(0, LANES), pl.ds(LANES, LANES)
 
     def scatter(kind, pick, target, columns):
-        copies = []
-        for distance in far_first:
-            copy = pltpu.make_async_remote_copy(
-                src_ref=pick(peer(distance)),
-                dst_ref=target.at[rows_of(me), columns],
-                send_sem=send_sem.at[kind, distance],
-                recv_sem=recv_sem.at[kind, distance],
-                device_id={"pipe": pipe, "seq": peer(distance)},
-                device_id_type=MESH,
-            )
+        sends, arrivals = [], []
+        for slot in range(last):
+            at = slot_peer(slot)
+            for index, copies in ((me, sends), (at, arrivals)):
+                copies.append(
+                    pltpu.make_async_remote_copy(
+                        src_ref=pick(at),
+                        dst_ref=target.at[rows_of(index), columns],
+                        send_sem=send_sem.at[kind, slot],
+                        recv_sem=recv_sem.at[kind, index],
+                        device_id={"pipe": pipe, "seq": at},
+                        device_id_type=MESH,
+                    )
+                )
+        for copy in sends[:-1]:
             copy.start()
-            copies.append(copy)
         own = pltpu.make_async_copy(
             pick(me), target.at[rows_of(me), columns], own_sem.at[kind]
         )
         own.start()
-        return own, copies
+        return own, sends, arrivals
 
     def landed(group):
-        own, copies = group
+        own, _, arrivals = group
         own.wait()
-        for copy in copies:
+        for copy in arrivals:
             copy.wait_recv()
 
     filt_group = scatter(0, lambda device: lf.at[0, :, lanes_of(device)], both_all, first)
@@ -288,6 +310,13 @@
     loads[1].wait()
     gate(qg, go, conv_src)
     conv_group = scatter(1, lambda device: conv_src.at[device], both_all, second)
+
+    @pl.when(jnp.logical_not(late))
+    def _():
+        pl.semaphore_wait(late_sem, 2)
+
+    filt_group[1][-1].start()
+    conv_group[1][-1].start()
     for copy in loads[4:]:
         copy.start()
     loads[2].wait()
@@ -309,6 +338,7 @@
         side.append(copy)
 
     gated_group = scatter(2, lambda device: gated_src.at[device], gated_all, first)
+    gated_group[1][-1].start()
     part = half // PARTS
 
     def transform(signal, target):
@@ -465,6 +495,7 @@
             pltpu.SemaphoreType.DMA((devices,)),
             pltpu.SemaphoreType.DMA((3,)),
             pltpu.SemaphoreType.DMA((3,)),
+            pltpu.SemaphoreType.REGULAR,
         ],
         compiler_params=pltpu.CompilerParams(
             collective_id=0, has_side_effects=True, vmem_limit_bytes=62 * 2**20

time: 36.6 us -> 37.1 us (1.014)
  Pallas kernels: 35.9 us -> 36.3 us
    pallas_call x1, Pallas kernels: 34.9 us -> 35.4 us  [relay_body(): pl.pallas_call(functools.partial(relay_kernel, devices), out_shape=(pltpu...]
where the time goes in v6:
time: 37.1 us; the launch traced here: 37 us
  Pallas kernels  36.3 us (98%)
  between operations  0.64 us (2%)
    pallas_call x1, Pallas kernels, relay_body(): pl.pallas_call(functools.partial(relay_kernel, devices), out_shape=(pltpu...  35.4 us
    pallas_call x1, Pallas kernels, relay_body(): pl.pallas_call(settle_kernel, out_shape=(jax.ShapeDtypeStruct(passed.shap...  0.94 us

profile of v6, /device:TPU:0, one launch (start us, length us, event | category | flops | bytes accessed | tf_op | source)
XLA Modules:
  0.0 37.0 jit_solution(11102798235811402173)
XLA Ops:
  0.6 35.4 %shard_map.95 = (bf16[1,256,512]{2,1,0:T(8,128)(2,1)S(1)}, f32[1,256,512]{2,1,0:T(8,128)S(1)}) custom-call(bf16[1,256,512]{2,1,0:T(8,128)(2,1)} %go_hbm.1, bf16[1,256,512]{2,1,0:T(8,128)(2,1)} %vb_hbm.1, bf16[1,256,512]{2,1,0:T(8,128)(2,1)} %kg_hbm.1, bf16[1,256,512]{2,1,0:T(8,128)(2,1)} %qg_hbm.1, f32[3,1,512]{2,1,0:T(1,128)} %bitcast.1, ...), custom_call_target="tpu_custom_call" | custom-call | flops 2147483648 | bytes 10485760 | tf_op jit(solution)/shard_map/pallas_call | solution.py:464
  36.0 0.9 %shard_map.96 = (bf16[1,256,512]{2,1,0:T(8,128)(2,1)}, f32[1,256,512]{2,1,0:T(8,128)}) custom-call(bf16[1,256,512]{2,1,0:T(8,128)(2,1)S(1)} %get-tuple-element.4.passed, f32[1,256,512]{2,1,0:T(8,128)S(1)} %get-tuple-element.5.fold), custom_call_target="tpu_custom_call" | custom-call | tf_op jit(solution)/shard_map/pallas_call | solution.py:510

commit v7 on v5

--- a/solution.py
+++ b/solution.py
@@ -223,7 +223,7 @@
         for block in range(devices):
             columns = pl.ds(block * LANES, LANES)
             value = left[:, columns].astype(jnp.float32) * right[:, columns].astype(jnp.float32)
-            target[block] = value.astype(jnp.bfloat16)
+            target[:, columns] = value.astype(jnp.bfloat16)
 
     def peer(distance):
         return lax.rem(me + distance, devices)
@@ -258,12 +258,12 @@
 
     first, second = pl.ds(0, LANES), pl.ds(LANES, LANES)
 
-    def scatter(kind, pick, target, columns):
+    def scatter(kind, pick, target):
         copies = []
         for distance in far_first:
             copy = pltpu.make_async_remote_copy(
                 src_ref=pick(peer(distance)),
-                dst_ref=target.at[rows_of(me), columns],
+                dst_ref=target.at[rows_of(me)],
                 send_sem=send_sem.at[kind, distance],
                 recv_sem=recv_sem.at[kind, distance],
                 device_id={"pipe": pipe, "seq": peer(distance)},
@@ -272,7 +272,7 @@
             copy.start()
             copies.append(copy)
         own = pltpu.make_async_copy(
-            pick(me), target.at[rows_of(me), columns], own_sem.at[kind]
+            pick(me), target.at[rows_of(me)], own_sem.at[kind]
         )
         own.start()
         return own, copies
@@ -283,11 +283,11 @@
         for copy in copies:
             copy.wait_recv()
 
-    filt_group = scatter(0, lambda device: lf.at[0, :, lanes_of(device)], both_all, first)
+    filt_group = scatter(0, lambda device: lf.at[0, :, lanes_of(device)], both_all.at[0])
     loads[0].wait()
     loads[1].wait()
     gate(qg, go, conv_src)
-    conv_group = scatter(1, lambda device: conv_src.at[device], both_all, second)
+    conv_group = scatter(1, lambda device: conv_src.at[:, lanes_of(device)], both_all.at[1])
     for copy in loads[4:]:
         copy.start()
     loads[2].wait()
@@ -308,14 +308,13 @@
         copy.start()
         side.append(copy)
 
-    gated_group = scatter(2, lambda device: gated_src.at[device], gated_all, first)
+    gated_group = scatter(2, lambda device: gated_src.at[:, lanes_of(device)], gated_all.at[0])
     part = half // PARTS
 
     def transform(signal, target):
-        width = signal.shape[1]
         evens, odds = [], []
-        for at in range(0, width, LANES):
-            mixed[...] = signal[:, pl.ds(at, LANES)].astype(jnp.float32)
+        for at in range(signal.shape[0]):
+            mixed[...] = signal[at].astype(jnp.float32)
             evens.append(mixed[pl.ds(0, half, stride=2), :].astype(jnp.bfloat16))
             odds.append(mixed[pl.ds(1, half, stride=2), :].astype(jnp.bfloat16))
         evens, odds = jnp.concatenate(evens, axis=1), jnp.concatenate(odds, axis=1)
@@ -439,11 +438,10 @@
         ),
         in_specs=[anywhere] * 8,
         out_specs=(vmem, vmem),
-        scratch_shapes=[pltpu.VMEM((rows, columns), half)] * 4
-        + [pltpu.VMEM((devices, rows, LANES), half)] * 2
+        scratch_shapes=[pltpu.VMEM((rows, columns), half)] * 6
         + [
-            pltpu.VMEM((tokens, 2 * LANES), half),
-            pltpu.VMEM((tokens, LANES), half),
+            pltpu.VMEM((2, tokens, LANES), half),
+            pltpu.VMEM((1, tokens, LANES), half),
             pltpu.VMEM(tables[0].shape, half),
             pltpu.VMEM(tables[1].shape, half),
             pltpu.VMEM((tokens, LANES), full),

time: 36.6 us -> 36.6 us (level)
  no operation moved by 1% of the time
where the time goes in v7:
time: 36.6 us; the launch traced here: 36.5 us
  Pallas kernels  35.9 us (98%)
  between operations  0.64 us (2%)
    pallas_call x1, Pallas kernels, relay_body(): pl.pallas_call(functools.partial(relay_kernel, devices), out_shape=(pltpu...  34.9 us
    pallas_call x1, Pallas kernels, relay_body(): pl.pallas_call(settle_kernel, out_shape=(jax.ShapeDtypeStruct(passed.shap...  0.94 us

profile of v7, /device:TPU:0, one launch (start us, length us, event | category | flops | bytes accessed | tf_op | source)
XLA Modules:
  0.0 36.5 jit_solution(3343586178429952113)
XLA Ops:
  0.6 34.9 %shard_map.95 = (bf16[1,256,512]{2,1,0:T(8,128)(2,1)S(1)}, f32[1,256,512]{2,1,0:T(8,128)S(1)}) custom-call(bf16[1,256,512]{2,1,0:T(8,128)(2,1)} %go_hbm.1, bf16[1,256,512]{2,1,0:T(8,128)(2,1)} %vb_hbm.1, bf16[1,256,512]{2,1,0:T(8,128)(2,1)} %kg_hbm.1, bf16[1,256,512]{2,1,0:T(8,128)(2,1)} %qg_hbm.1, f32[3,1,512]{2,1,0:T(1,128)} %bitcast.1, ...), custom_call_target="tpu_custom_call" | custom-call | flops 2147483648 | bytes 10485760 | tf_op jit(solution)/shard_map/pallas_call | solution.py:433
  35.6 0.9 %shard_map.96 = (bf16[1,256,512]{2,1,0:T(8,128)(2,1)}, f32[1,256,512]{2,1,0:T(8,128)}) custom-call(bf16[1,256,512]{2,1,0:T(8,128)(2,1)S(1)} %get-tuple-element.4.passed, f32[1,256,512]{2,1,0:T(8,128)S(1)} %get-tuple-element.5.fold), custom_call_target="tpu_custom_call" | custom-call | tf_op jit(solution)/shard_map/pallas_call | solution.py:477
